TPU v7x, 32 devices: a whole 2x2x4 slice. The times are simulated.
32 devices in a mesh: grp: 2 (over y), res: 8 (over z, x), ta: 2 (over core).
Axes of the slice: x: 2, y: 2, z: 4, core: 2. Of those that a mesh axis runs over, the one named last changes fastest.
Arguments:
- log_order: int32 [8, 512], P('res'), may hold values from 1 to 4096, as said below
- t_start: int32 [2], P('grp'), parts along dimension 0, may hold values from 160 to 319
- term_counts: int32 [1024], P(('grp', 'ta')), parts along dimension 0, may hold values from 4 to 32, as said below
Outputs:
- refined: float32 [2, 8, 512, 2048], P(None, None, 'res', ('grp', 'ta')), parts along dimension 3
There are 2 independent parts, one for each index of `grp`. A program takes and returns all parts, laid end to end along the dimension named above; an argument that names none is the same for every part. Nothing has to cross between parts.
Inputs may be any that keep to these rules, and one draw needn't show every extreme that they name: `log_order`: every residue 1 to 4096 appears once. `term_counts`: at least an eighth of t_m plus two, except at the first point.
All inputs are finite; a program needn't handle non-finite values.
Results may differ from a plain program's by a relative error of at most 0.00023.
Values sent between devices are 32-bit elements; how exact they have to be, the bound alone decides.
A program may use at most 64 MiB of HBM per device.

v0:
```python
import math
import jax
import jax.numpy as jnp
from jax import lax
from jax.sharding import PartitionSpec as P

TAPS = 8
MAXN = 32
time_step = 0.0625


def padded_2(block, sides, width):
    for axis, dim in sides:
        count = lax.axis_size(axis)
        forward = [(i, i + 1) for i in range(count - 1)]
        backward = [(target, source) for source, target in forward]
        low = lax.ppermute(
            lax.slice_in_dim(block, block.shape[dim] - width, None, axis=dim), axis, forward
        )
        high = lax.ppermute(lax.slice_in_dim(block, 0, width, axis=dim), axis, backward)
        block = jnp.concatenate([low, block, high], axis=dim)
    return block


def inverse_power(base_value, t_values):
    modulus = lax.rsqrt(base_value)
    phase_now = t_values * jnp.log(base_value)
    return (modulus * jnp.cos(phase_now), -modulus * jnp.sin(phase_now))


def hurwitz_values(x_values, t_values, count_row, most_terms):
    shape_out = (x_values.shape[0], t_values.shape[1])

    def add_term(term_index, running):
        sum_re, sum_im = running
        base_value = term_index.astype(x_values.dtype) + x_values
        piece_re, piece_im = inverse_power(base_value, t_values)
        active = term_index < count_row
        return (
            sum_re + jnp.where(active, piece_re, 0.0),
            sum_im + jnp.where(active, piece_im, 0.0),
        )

    zeros_init = jnp.zeros(shape_out, x_values.dtype)
    sum_re, sum_im = lax.fori_loop(0, most_terms, add_term, (zeros_init, zeros_init))
    tail_base = count_row.astype(x_values.dtype) + x_values
    power_re, power_im = inverse_power(tail_base, t_values)
    denominator = 0.25 + t_values * t_values
    lifted_re = tail_base * power_re
    lifted_im = tail_base * power_im
    total_re = sum_re + (-0.5 * lifted_re + t_values * lifted_im) / denominator + 0.5 * power_re
    total_im = sum_im + (-t_values * lifted_re - 0.5 * lifted_im) / denominator + 0.5 * power_im
    total_re = total_re + (0.5 * power_re - t_values * power_im) / (12.0 * tail_base)
    total_im = total_im + (0.5 * power_im + t_values * power_re) / (12.0 * tail_base)
    cubic_re = 1.875 - 4.5 * t_values * t_values
    cubic_im = 5.75 * t_values - t_values * t_values * t_values
    cube_base = 720.0 * tail_base * tail_base * tail_base
    total_re = total_re - (cubic_re * power_re - cubic_im * power_im) / cube_base
    total_im = total_im - (cubic_re * power_im + cubic_im * power_re) / cube_base
    return (total_re, total_im)


def sinc_value(offset):
    return math.sin(math.pi * offset) / (math.pi * offset)


def refine(padded, half_width, length):
    coarse = padded[..., half_width : half_width + length]
    middle = jnp.zeros_like(coarse)
    for offset in range(1 - half_width, half_width + 1):
        weight = sinc_value(offset - 0.5) * sinc_value((offset - 0.5) / half_width)
        middle = middle + weight * padded[..., half_width + offset : half_width + offset + length]
    stacked = jnp.stack([coarse, middle], axis=-1)
    return stacked.reshape(stacked.shape[:-2] + (2 * length,))


def matmul_high(left, right):
    return jnp.dot(left, right, precision=lax.Precision.HIGHEST, preferred_element_type=jnp.float32)


def per_device(log_order, t_start, term_counts):
    rows_here = log_order.shape[1]
    slabs = lax.axis_size("res")
    slab_index = lax.axis_index("res")
    length_here = term_counts.shape[0]
    ta_index = lax.axis_index("ta")
    modulus_int = slabs * rows_here + 1
    x_values = log_order.reshape(rows_here, 1).astype(jnp.float32) / jnp.float32(modulus_int)
    row_ids = jnp.arange(rows_here, dtype=jnp.int32)
    first_phase = (row_ids[:, None] * row_ids[None, :] % rows_here).astype(jnp.float32) * (
        2.0 * math.pi / rows_here
    )
    first_cos = jnp.cos(first_phase)
    first_sin = jnp.sin(first_phase)
    twist_phase = (row_ids * slab_index).astype(jnp.float32)[:, None] * (
        2.0 * math.pi / (slabs * rows_here)
    )
    twist_cos = jnp.cos(twist_phase)
    twist_sin = jnp.sin(twist_phase)
    slab_ids = jnp.arange(slabs, dtype=jnp.int32)
    second_phase = (slab_ids[:, None] * slab_ids[None, :] % slabs).astype(jnp.float32) * (
        2.0 * math.pi / slabs
    )
    second_cos = jnp.cos(second_phase)
    second_sin = jnp.sin(second_phase)
    positions = ta_index * length_here + jnp.arange(length_here, dtype=jnp.int32)
    count_row = term_counts[None, :]
    t_values = ((t_start[0] + positions).astype(jnp.float32) * time_step)[None, :]
    zeta_re, zeta_im = hurwitz_values(x_values, t_values, count_row, MAXN)
    mixed_re = matmul_high(first_cos, zeta_re) - matmul_high(first_sin, zeta_im)
    mixed_im = matmul_high(first_sin, zeta_re) + matmul_high(first_cos, zeta_im)
    turned_re = twist_cos * mixed_re - twist_sin * mixed_im
    turned_im = twist_sin * mixed_re + twist_cos * mixed_im
    sectioned = jnp.stack([turned_re, turned_im])[:, None]
    block_in = lax.all_to_all(sectioned, "res", split_axis=2, concat_axis=1, tiled=True)
    part_re = block_in[0]
    part_im = block_in[1]

    def mix(table, values):
        return jnp.einsum(
            "wp,psn->wsn",
            table,
            values,
            precision=lax.Precision.HIGHEST,
            preferred_element_type=jnp.float32,
        )

    out_re = mix(second_cos, part_re) - mix(second_sin, part_im)
    out_im = mix(second_sin, part_re) + mix(second_cos, part_im)
    spectrum = jnp.stack([out_re, out_im])
    factor_re, factor_im = inverse_power(jnp.float32(modulus_int), t_values)
    lval_re = spectrum[0] * factor_re - spectrum[1] * factor_im
    lval_im = spectrum[0] * factor_im + spectrum[1] * factor_re
    lvals = jnp.stack([lval_re, lval_im])
    padded = padded_2(lvals, (("ta", 3),), TAPS)
    return refine(padded, TAPS, length_here)


def solution(mesh):
    placed = (P("res", None), P("grp"), P(("grp", "ta")))
    return jax.shard_map(
        per_device,
        mesh=mesh,
        in_specs=placed,
        out_specs=P(None, None, "res", ("grp", "ta")),
        check_vma=False,
    )
```

profile of v0, /device:TPU:0, one launch (start us, length us, event | category | flops | bytes accessed | tf_op | source)
XLA Modules:
  0.0 207.3 jit_solution(16231159181828599554)
XLA Ops:
  2.1 121.0 %while.16 = (s32[]{:T(128)}, f32[512,256]{1,0:T(8,128)S(1)}, f32[512,256]{1,0:T(8,128)S(1)}, s32[1,256]{1,0:T(1,128)}, f32[512,1]{0,1:T(1,128)S(1)}, /*index=5*/s32[]{:T(128)}, s32[]{:T(128)}, s32[]{:T(128)}, s32[]{:T(128)}) while((s32[]{:T(128)}, f32[512,256]{1,0:T(8,128)S(1)}, f32[512,256]{1,0:T(8,128)S(1)}, s32[1,256]{1,0:T(1,128)}, ...), condition=%wide.region_1.2_spmd.clone, body=%wide.region_0.1_spmd.clone.sunk | while | flops 1181956 | bytes 2117255 | solution.py:45
  3.4 2.4 %fusion.139 = (f32[512,256]{1,0:T(8,128)S(1)}, f32[512,256]{1,0:T(8,128)S(1)}) fusion(f32[512,256]{1,0:T(8,128)S(1)} %get-tuple-element.249, f32[512]{0:T(512)S(1)} %neg.53, f32[512]{0:T(512)S(1)} %bitcast.58, f32[256]{0:T(256)S(1)} %bitcast.59, pred[]{:T(512)S(6)} %compare.5, pred[256]{0:T(512)(128)(4,1)S(1)} %compare_reduce_fusion.2, ...), kind=kLoop, calls=%fused_computation.8.clone.1 | loop fusion | flops 1179648 | bytes 2104577 | tf_op jit(solution)/shard_map/while/body/eval_jaxpr/add | solution.py:41
  5.8 0.7 compare_reduce_fusion.2
  7.2 2.4 %fusion.139 = (f32[512,256]{1,0:T(8,128)S(1)}, f32[512,256]{1,0:T(8,128)S(1)}) fusion(f32[512,256]{1,0:T(8,128)S(1)} %get-tuple-element.249, f32[512]{0:T(512)S(1)} %neg.53, f32[512]{0:T(512)S(1)} %bitcast.58, f32[256]{0:T(256)S(1)} %bitcast.59, pred[]{:T(512)S(6)} %compare.5, pred[256]{0:T(512)(128)(4,1)S(1)} %compare_reduce_fusion.2, ...), kind=kLoop, calls=%fused_computation.8.clone.1 | loop fusion | flops 1179648 | bytes 2104577 | tf_op jit(solution)/shard_map/while/body/eval_jaxpr/add | solution.py:41
  9.6 0.7 compare_reduce_fusion.2
  11.0 2.4 %fusion.139 = (f32[512,256]{1,0:T(8,128)S(1)}, f32[512,256]{1,0:T(8,128)S(1)}) fusion(f32[512,256]{1,0:T(8,128)S(1)} %get-tuple-element.249, f32[512]{0:T(512)S(1)} %neg.53, f32[512]{0:T(512)S(1)} %bitcast.58, f32[256]{0:T(256)S(1)} %bitcast.59, pred[]{:T(512)S(6)} %compare.5, pred[256]{0:T(512)(128)(4,1)S(1)} %compare_reduce_fusion.2, ...), kind=kLoop, calls=%fused_computation.8.clone.1 | loop fusion | flops 1179648 | bytes 2104577 | tf_op jit(solution)/shard_map/while/body/eval_jaxpr/add | solution.py:41
  13.4 0.7 compare_reduce_fusion.2
  14.8 2.4 %fusion.139 = (f32[512,256]{1,0:T(8,128)S(1)}, f32[512,256]{1,0:T(8,128)S(1)}) fusion(f32[512,256]{1,0:T(8,128)S(1)} %get-tuple-element.249, f32[512]{0:T(512)S(1)} %neg.53, f32[512]{0:T(512)S(1)} %bitcast.58, f32[256]{0:T(256)S(1)} %bitcast.59, pred[]{:T(512)S(6)} %compare.5, pred[256]{0:T(512)(128)(4,1)S(1)} %compare_reduce_fusion.2, ...), kind=kLoop, calls=%fused_computation.8.clone.1 | loop fusion | flops 1179648 | bytes 2104577 | tf_op jit(solution)/shard_map/while/body/eval_jaxpr/add | solution.py:41
  18.6 2.4 %fusion.139 = (f32[512,256]{1,0:T(8,128)S(1)}, f32[512,256]{1,0:T(8,128)S(1)}) fusion(f32[512,256]{1,0:T(8,128)S(1)} %get-tuple-element.249, f32[512]{0:T(512)S(1)} %neg.53, f32[512]{0:T(512)S(1)} %bitcast.58, f32[256]{0:T(256)S(1)} %bitcast.59, pred[]{:T(512)S(6)} %compare.5, pred[256]{0:T(512)(128)(4,1)S(1)} %compare_reduce_fusion.2, ...), kind=kLoop, calls=%fused_computation.8.clone.1 | loop fusion | flops 1179648 | bytes 2104577 | tf_op jit(solution)/shard_map/while/body/eval_jaxpr/add | solution.py:41
  21.0 0.7 compare_reduce_fusion.2
  22.4 2.4 %fusion.139 = (f32[512,256]{1,0:T(8,128)S(1)}, f32[512,256]{1,0:T(8,128)S(1)}) fusion(f32[512,256]{1,0:T(8,128)S(1)} %get-tuple-element.249, f32[512]{0:T(512)S(1)} %neg.53, f32[512]{0:T(512)S(1)} %bitcast.58, f32[256]{0:T(256)S(1)} %bitcast.59, pred[]{:T(512)S(6)} %compare.5, pred[256]{0:T(512)(128)(4,1)S(1)} %compare_reduce_fusion.2, ...), kind=kLoop, calls=%fused_computation.8.clone.1 | loop fusion | flops 1179648 | bytes 2104577 | tf_op jit(solution)/shard_map/while/body/eval_jaxpr/add | solution.py:41
  26.1 2.4 %fusion.139 = (f32[512,256]{1,0:T(8,128)S(1)}, f32[512,256]{1,0:T(8,128)S(1)}) fusion(f32[512,256]{1,0:T(8,128)S(1)} %get-tuple-element.249, f32[512]{0:T(512)S(1)} %neg.53, f32[512]{0:T(512)S(1)} %bitcast.58, f32[256]{0:T(256)S(1)} %bitcast.59, pred[]{:T(512)S(6)} %compare.5, pred[256]{0:T(512)(128)(4,1)S(1)} %compare_reduce_fusion.2, ...), kind=kLoop, calls=%fused_computation.8.clone.1 | loop fusion | flops 1179648 | bytes 2104577 | tf_op jit(solution)/shard_map/while/body/eval_jaxpr/add | solution.py:41
  29.9 2.4 %fusion.139 = (f32[512,256]{1,0:T(8,128)S(1)}, f32[512,256]{1,0:T(8,128)S(1)}) fusion(f32[512,256]{1,0:T(8,128)S(1)} %get-tuple-element.249, f32[512]{0:T(512)S(1)} %neg.53, f32[512]{0:T(512)S(1)} %bitcast.58, f32[256]{0:T(256)S(1)} %bitcast.59, pred[]{:T(512)S(6)} %compare.5, pred[256]{0:T(512)(128)(4,1)S(1)} %compare_reduce_fusion.2, ...), kind=kLoop, calls=%fused_computation.8.clone.1 | loop fusion | flops 1179648 | bytes 2104577 | tf_op jit(solution)/shard_map/while/body/eval_jaxpr/add | solution.py:41
  33.7 2.4 %fusion.139 = (f32[512,256]{1,0:T(8,128)S(1)}, f32[512,256]{1,0:T(8,128)S(1)}) fusion(f32[512,256]{1,0:T(8,128)S(1)} %get-tuple-element.249, f32[512]{0:T(512)S(1)} %neg.53, f32[512]{0:T(512)S(1)} %bitcast.58, f32[256]{0:T(256)S(1)} %bitcast.59, pred[]{:T(512)S(6)} %compare.5, pred[256]{0:T(512)(128)(4,1)S(1)} %compare_reduce_fusion.2, ...), kind=kLoop, calls=%fused_computation.8.clone.1 | loop fusion | flops 1179648 | bytes 2104577 | tf_op jit(solution)/shard_map/while/body/eval_jaxpr/add | solution.py:41
  37.5 2.4 %fusion.139 = (f32[512,256]{1,0:T(8,128)S(1)}, f32[512,256]{1,0:T(8,128)S(1)}) fusion(f32[512,256]{1,0:T(8,128)S(1)} %get-tuple-element.249, f32[512]{0:T(512)S(1)} %neg.53, f32[512]{0:T(512)S(1)} %bitcast.58, f32[256]{0:T(256)S(1)} %bitcast.59, pred[]{:T(512)S(6)} %compare.5, pred[256]{0:T(512)(128)(4,1)S(1)} %compare_reduce_fusion.2, ...), kind=kLoop, calls=%fused_computation.8.clone.1 | loop fusion | flops 1179648 | bytes 2104577 | tf_op jit(solution)/shard_map/while/body/eval_jaxpr/add | solution.py:41
  39.9 0.7 compare_reduce_fusion.2
  41.3 2.4 %fusion.139 = (f32[512,256]{1,0:T(8,128)S(1)}, f32[512,256]{1,0:T(8,128)S(1)}) fusion(f32[512,256]{1,0:T(8,128)S(1)} %get-tuple-element.249, f32[512]{0:T(512)S(1)} %neg.53, f32[512]{0:T(512)S(1)} %bitcast.58, f32[256]{0:T(256)S(1)} %bitcast.59, pred[]{:T(512)S(6)} %compare.5, pred[256]{0:T(512)(128)(4,1)S(1)} %compare_reduce_fusion.2, ...), kind=kLoop, calls=%fused_computation.8.clone.1 | loop fusion | flops 1179648 | bytes 2104577 | tf_op jit(solution)/shard_map/while/body/eval_jaxpr/add | solution.py:41
  45.1 2.4 %fusion.139 = (f32[512,256]{1,0:T(8,128)S(1)}, f32[512,256]{1,0:T(8,128)S(1)}) fusion(f32[512,256]{1,0:T(8,128)S(1)} %get-tuple-element.249, f32[512]{0:T(512)S(1)} %neg.53, f32[512]{0:T(512)S(1)} %bitcast.58, f32[256]{0:T(256)S(1)} %bitcast.59, pred[]{:T(512)S(6)} %compare.5, pred[256]{0:T(512)(128)(4,1)S(1)} %compare_reduce_fusion.2, ...), kind=kLoop, calls=%fused_computation.8.clone.1 | loop fusion | flops 1179648 | bytes 2104577 | tf_op jit(solution)/shard_map/while/body/eval_jaxpr/add | solution.py:41
  47.4 0.7 compare_reduce_fusion.2
  48.8 2.4 %fusion.139 = (f32[512,256]{1,0:T(8,128)S(1)}, f32[512,256]{1,0:T(8,128)S(1)}) fusion(f32[512,256]{1,0:T(8,128)S(1)} %get-tuple-element.249, f32[512]{0:T(512)S(1)} %neg.53, f32[512]{0:T(512)S(1)} %bitcast.58, f32[256]{0:T(256)S(1)} %bitcast.59, pred[]{:T(512)S(6)} %compare.5, pred[256]{0:T(512)(128)(4,1)S(1)} %compare_reduce_fusion.2, ...), kind=kLoop, calls=%fused_computation.8.clone.1 | loop fusion | flops 1179648 | bytes 2104577 | tf_op jit(solution)/shard_map/while/body/eval_jaxpr/add | solution.py:41
  52.6 2.4 %fusion.139 = (f32[512,256]{1,0:T(8,128)S(1)}, f32[512,256]{1,0:T(8,128)S(1)}) fusion(f32[512,256]{1,0:T(8,128)S(1)} %get-tuple-element.249, f32[512]{0:T(512)S(1)} %neg.53, f32[512]{0:T(512)S(1)} %bitcast.58, f32[256]{0:T(256)S(1)} %bitcast.59, pred[]{:T(512)S(6)} %compare.5, pred[256]{0:T(512)(128)(4,1)S(1)} %compare_reduce_fusion.2, ...), kind=kLoop, calls=%fused_computation.8.clone.1 | loop fusion | flops 1179648 | bytes 2104577 | tf_op jit(solution)/shard_map/while/body/eval_jaxpr/add | solution.py:41
  56.4 2.4 %fusion.139 = (f32[512,256]{1,0:T(8,128)S(1)}, f32[512,256]{1,0:T(8,128)S(1)}) fusion(f32[512,256]{1,0:T(8,128)S(1)} %get-tuple-element.249, f32[512]{0:T(512)S(1)} %neg.53, f32[512]{0:T(512)S(1)} %bitcast.58, f32[256]{0:T(256)S(1)} %bitcast.59, pred[]{:T(512)S(6)} %compare.5, pred[256]{0:T(512)(128)(4,1)S(1)} %compare_reduce_fusion.2, ...), kind=kLoop, calls=%fused_computation.8.clone.1 | loop fusion | flops 1179648 | bytes 2104577 | tf_op jit(solution)/shard_map/while/body/eval_jaxpr/add | solution.py:41
  58.8 0.7 compare_reduce_fusion.2
  60.2 2.4 %fusion.139 = (f32[512,256]{1,0:T(8,128)S(1)}, f32[512,256]{1,0:T(8,128)S(1)}) fusion(f32[512,256]{1,0:T(8,128)S(1)} %get-tuple-element.249, f32[512]{0:T(512)S(1)} %neg.53, f32[512]{0:T(512)S(1)} %bitcast.58, f32[256]{0:T(256)S(1)} %bitcast.59, pred[]{:T(512)S(6)} %compare.5, pred[256]{0:T(512)(128)(4,1)S(1)} %compare_reduce_fusion.2, ...), kind=kLoop, calls=%fused_computation.8.clone.1 | loop fusion | flops 1179648 | bytes 2104577 | tf_op jit(solution)/shard_map/while/body/eval_jaxpr/add | solution.py:41
  64.0 2.4 %fusion.139 = (f32[512,256]{1,0:T(8,128)S(1)}, f32[512,256]{1,0:T(8,128)S(1)}) fusion(f32[512,256]{1,0:T(8,128)S(1)} %get-tuple-element.249, f32[512]{0:T(512)S(1)} %neg.53, f32[512]{0:T(512)S(1)} %bitcast.58, f32[256]{0:T(256)S(1)} %bitcast.59, pred[]{:T(512)S(6)} %compare.5, pred[256]{0:T(512)(128)(4,1)S(1)} %compare_reduce_fusion.2, ...), kind=kLoop, calls=%fused_computation.8.clone.1 | loop fusion | flops 1179648 | bytes 2104577 | tf_op jit(solution)/shard_map/while/body/eval_jaxpr/add | solution.py:41
  66.4 0.7 compare_reduce_fusion.2
  67.8 2.4 %fusion.139 = (f32[512,256]{1,0:T(8,128)S(1)}, f32[512,256]{1,0:T(8,128)S(1)}) fusion(f32[512,256]{1,0:T(8,128)S(1)} %get-tuple-element.249, f32[512]{0:T(512)S(1)} %neg.53, f32[512]{0:T(512)S(1)} %bitcast.58, f32[256]{0:T(256)S(1)} %bitcast.59, pred[]{:T(512)S(6)} %compare.5, pred[256]{0:T(512)(128)(4,1)S(1)} %compare_reduce_fusion.2, ...), kind=kLoop, calls=%fused_computation.8.clone.1 | loop fusion | flops 1179648 | bytes 2104577 | tf_op jit(solution)/shard_map/while/body/eval_jaxpr/add | solution.py:41
  71.5 2.4 %fusion.139 = (f32[512,256]{1,0:T(8,128)S(1)}, f32[512,256]{1,0:T(8,128)S(1)}) fusion(f32[512,256]{1,0:T(8,128)S(1)} %get-tuple-element.249, f32[512]{0:T(512)S(1)} %neg.53, f32[512]{0:T(512)S(1)} %bitcast.58, f32[256]{0:T(256)S(1)} %bitcast.59, pred[]{:T(512)S(6)} %compare.5, pred[256]{0:T(512)(128)(4,1)S(1)} %compare_reduce_fusion.2, ...), kind=kLoop, calls=%fused_computation.8.clone.1 | loop fusion | flops 1179648 | bytes 2104577 | tf_op jit(solution)/shard_map/while/body/eval_jaxpr/add | solution.py:41
  75.3 2.4 %fusion.139 = (f32[512,256]{1,0:T(8,128)S(1)}, f32[512,256]{1,0:T(8,128)S(1)}) fusion(f32[512,256]{1,0:T(8,128)S(1)} %get-tuple-element.249, f32[512]{0:T(512)S(1)} %neg.53, f32[512]{0:T(512)S(1)} %bitcast.58, f32[256]{0:T(256)S(1)} %bitcast.59, pred[]{:T(512)S(6)} %compare.5, pred[256]{0:T(512)(128)(4,1)S(1)} %compare_reduce_fusion.2, ...), kind=kLoop, calls=%fused_computation.8.clone.1 | loop fusion | flops 1179648 | bytes 2104577 | tf_op jit(solution)/shard_map/while/body/eval_jaxpr/add | solution.py:41
  79.1 2.4 %fusion.139 = (f32[512,256]{1,0:T(8,128)S(1)}, f32[512,256]{1,0:T(8,128)S(1)}) fusion(f32[512,256]{1,0:T(8,128)S(1)} %get-tuple-element.249, f32[512]{0:T(512)S(1)} %neg.53, f32[512]{0:T(512)S(1)} %bitcast.58, f32[256]{0:T(256)S(1)} %bitcast.59, pred[]{:T(512)S(6)} %compare.5, pred[256]{0:T(512)(128)(4,1)S(1)} %compare_reduce_fusion.2, ...), kind=kLoop, calls=%fused_computation.8.clone.1 | loop fusion | flops 1179648 | bytes 2104577 | tf_op jit(solution)/shard_map/while/body/eval_jaxpr/add | solution.py:41
  82.9 2.4 %fusion.139 = (f32[512,256]{1,0:T(8,128)S(1)}, f32[512,256]{1,0:T(8,128)S(1)}) fusion(f32[512,256]{1,0:T(8,128)S(1)} %get-tuple-element.249, f32[512]{0:T(512)S(1)} %neg.53, f32[512]{0:T(512)S(1)} %bitcast.58, f32[256]{0:T(256)S(1)} %bitcast.59, pred[]{:T(512)S(6)} %compare.5, pred[256]{0:T(512)(128)(4,1)S(1)} %compare_reduce_fusion.2, ...), kind=kLoop, calls=%fused_computation.8.clone.1 | loop fusion | flops 1179648 | bytes 2104577 | tf_op jit(solution)/shard_map/while/body/eval_jaxpr/add | solution.py:41
  85.3 0.7 compare_reduce_fusion.2
  86.7 2.4 %fusion.139 = (f32[512,256]{1,0:T(8,128)S(1)}, f32[512,256]{1,0:T(8,128)S(1)}) fusion(f32[512,256]{1,0:T(8,128)S(1)} %get-tuple-element.249, f32[512]{0:T(512)S(1)} %neg.53, f32[512]{0:T(512)S(1)} %bitcast.58, f32[256]{0:T(256)S(1)} %bitcast.59, pred[]{:T(512)S(6)} %compare.5, pred[256]{0:T(512)(128)(4,1)S(1)} %compare_reduce_fusion.2, ...), kind=kLoop, calls=%fused_computation.8.clone.1 | loop fusion | flops 1179648 | bytes 2104577 | tf_op jit(solution)/shard_map/while/body/eval_jaxpr/add | solution.py:41
  90.4 2.4 %fusion.139 = (f32[512,256]{1,0:T(8,128)S(1)}, f32[512,256]{1,0:T(8,128)S(1)}) fusion(f32[512,256]{1,0:T(8,128)S(1)} %get-tuple-element.249, f32[512]{0:T(512)S(1)} %neg.53, f32[512]{0:T(512)S(1)} %bitcast.58, f32[256]{0:T(256)S(1)} %bitcast.59, pred[]{:T(512)S(6)} %compare.5, pred[256]{0:T(512)(128)(4,1)S(1)} %compare_reduce_fusion.2, ...), kind=kLoop, calls=%fused_computation.8.clone.1 | loop fusion | flops 1179648 | bytes 2104577 | tf_op jit(solution)/shard_map/while/body/eval_jaxpr/add | solution.py:41
  92.8 0.7 compare_reduce_fusion.2
  94.2 2.4 %fusion.139 = (f32[512,256]{1,0:T(8,128)S(1)}, f32[512,256]{1,0:T(8,128)S(1)}) fusion(f32[512,256]{1,0:T(8,128)S(1)} %get-tuple-element.249, f32[512]{0:T(512)S(1)} %neg.53, f32[512]{0:T(512)S(1)} %bitcast.58, f32[256]{0:T(256)S(1)} %bitcast.59, pred[]{:T(512)S(6)} %compare.5, pred[256]{0:T(512)(128)(4,1)S(1)} %compare_reduce_fusion.2, ...), kind=kLoop, calls=%fused_computation.8.clone.1 | loop fusion | flops 1179648 | bytes 2104577 | tf_op jit(solution)/shard_map/while/body/eval_jaxpr/add | solution.py:41
  98.0 2.4 %fusion.139 = (f32[512,256]{1,0:T(8,128)S(1)}, f32[512,256]{1,0:T(8,128)S(1)}) fusion(f32[512,256]{1,0:T(8,128)S(1)} %get-tuple-element.249, f32[512]{0:T(512)S(1)} %neg.53, f32[512]{0:T(512)S(1)} %bitcast.58, f32[256]{0:T(256)S(1)} %bitcast.59, pred[]{:T(512)S(6)} %compare.5, pred[256]{0:T(512)(128)(4,1)S(1)} %compare_reduce_fusion.2, ...), kind=kLoop, calls=%fused_computation.8.clone.1 | loop fusion | flops 1179648 | bytes 2104577 | tf_op jit(solution)/shard_map/while/body/eval_jaxpr/add | solution.py:41
  101.8 2.4 %fusion.139 = (f32[512,256]{1,0:T(8,128)S(1)}, f32[512,256]{1,0:T(8,128)S(1)}) fusion(f32[512,256]{1,0:T(8,128)S(1)} %get-tuple-element.249, f32[512]{0:T(512)S(1)} %neg.53, f32[512]{0:T(512)S(1)} %bitcast.58, f32[256]{0:T(256)S(1)} %bitcast.59, pred[]{:T(512)S(6)} %compare.5, pred[256]{0:T(512)(128)(4,1)S(1)} %compare_reduce_fusion.2, ...), kind=kLoop, calls=%fused_computation.8.clone.1 | loop fusion | flops 1179648 | bytes 2104577 | tf_op jit(solution)/shard_map/while/body/eval_jaxpr/add | solution.py:41
  105.6 2.4 %fusion.139 = (f32[512,256]{1,0:T(8,128)S(1)}, f32[512,256]{1,0:T(8,128)S(1)}) fusion(f32[512,256]{1,0:T(8,128)S(1)} %get-tuple-element.249, f32[512]{0:T(512)S(1)} %neg.53, f32[512]{0:T(512)S(1)} %bitcast.58, f32[256]{0:T(256)S(1)} %bitcast.59, pred[]{:T(512)S(6)} %compare.5, pred[256]{0:T(512)(128)(4,1)S(1)} %compare_reduce_fusion.2, ...), kind=kLoop, calls=%fused_computation.8.clone.1 | loop fusion | flops 1179648 | bytes 2104577 | tf_op jit(solution)/shard_map/while/body/eval_jaxpr/add | solution.py:41
  109.4 2.4 %fusion.139 = (f32[512,256]{1,0:T(8,128)S(1)}, f32[512,256]{1,0:T(8,128)S(1)}) fusion(f32[512,256]{1,0:T(8,128)S(1)} %get-tuple-element.249, f32[512]{0:T(512)S(1)} %neg.53, f32[512]{0:T(512)S(1)} %bitcast.58, f32[256]{0:T(256)S(1)} %bitcast.59, pred[]{:T(512)S(6)} %compare.5, pred[256]{0:T(512)(128)(4,1)S(1)} %compare_reduce_fusion.2, ...), kind=kLoop, calls=%fused_computation.8.clone.1 | loop fusion | flops 1179648 | bytes 2104577 | tf_op jit(solution)/shard_map/while/body/eval_jaxpr/add | solution.py:41
  111.8 0.7 compare_reduce_fusion.2
  113.1 2.4 %fusion.139 = (f32[512,256]{1,0:T(8,128)S(1)}, f32[512,256]{1,0:T(8,128)S(1)}) fusion(f32[512,256]{1,0:T(8,128)S(1)} %get-tuple-element.249, f32[512]{0:T(512)S(1)} %neg.53, f32[512]{0:T(512)S(1)} %bitcast.58, f32[256]{0:T(256)S(1)} %bitcast.59, pred[]{:T(512)S(6)} %compare.5, pred[256]{0:T(512)(128)(4,1)S(1)} %compare_reduce_fusion.2, ...), kind=kLoop, calls=%fused_computation.8.clone.1 | loop fusion | flops 1179648 | bytes 2104577 | tf_op jit(solution)/shard_map/while/body/eval_jaxpr/add | solution.py:41
  116.9 2.4 %fusion.139 = (f32[512,256]{1,0:T(8,128)S(1)}, f32[512,256]{1,0:T(8,128)S(1)}) fusion(f32[512,256]{1,0:T(8,128)S(1)} %get-tuple-element.249, f32[512]{0:T(512)S(1)} %neg.53, f32[512]{0:T(512)S(1)} %bitcast.58, f32[256]{0:T(256)S(1)} %bitcast.59, pred[]{:T(512)S(6)} %compare.5, pred[256]{0:T(512)(128)(4,1)S(1)} %compare_reduce_fusion.2, ...), kind=kLoop, calls=%fused_computation.8.clone.1 | loop fusion | flops 1179648 | bytes 2104577 | tf_op jit(solution)/shard_map/while/body/eval_jaxpr/add | solution.py:41
  119.3 0.7 compare_reduce_fusion.2
  120.7 2.4 %fusion.139 = (f32[512,256]{1,0:T(8,128)S(1)}, f32[512,256]{1,0:T(8,128)S(1)}) fusion(f32[512,256]{1,0:T(8,128)S(1)} %get-tuple-element.249, f32[512]{0:T(512)S(1)} %neg.53, f32[512]{0:T(512)S(1)} %bitcast.58, f32[256]{0:T(256)S(1)} %bitcast.59, pred[]{:T(512)S(6)} %compare.5, pred[256]{0:T(512)(128)(4,1)S(1)} %compare_reduce_fusion.2, ...), kind=kLoop, calls=%fused_computation.8.clone.1 | loop fusion | flops 1179648 | bytes 2104577 | tf_op jit(solution)/shard_map/while/body/eval_jaxpr/add | solution.py:41
  123.1 2.9 %fusion.38 = (f32[512,256]{1,0:T(8,128)S(1)}, f32[512,256]{1,0:T(8,128)S(1)}) fusion(f32[512,256]{1,0:T(8,128)S(1)} %get-tuple-element.116, f32[256]{0:T(256)S(1)} %fusion.93, f32[256]{0:T(256)S(1)} %get-tuple-element.180, f32[256]{0:T(256)S(1)} %get-tuple-element.183, f32[256]{0:T(256)S(1)} %get-tuple-element.179, f32[256]{0:T(256)S(1)} %get-tuple-element.184, ...), kind=kLoop, calls=%fused_computation.82 | loop fusion | flops 5636096 | bytes 2105344 | tf_op jit(solution)/shard_map/sub | solution.py:59
  126.0 5.6 %fusion.65 = f32[512,256]{1,0:T(8,128)S(1)} fusion(f32[512,256]{1,0:T(8,128)S(1)} %get-tuple-element.176), kind=kOutput, calls=%fused_computation.111 | convolution fusion | flops 808976384 | bytes 1048576 | tf_op jit(solution)/shard_map/dot_general | solution.py:78
  131.6 5.6 %fusion.63 = f32[512,256]{1,0:T(8,128)S(1)} fusion(f32[512,256]{1,0:T(8,128)S(1)} %get-tuple-element.176), kind=kOutput, calls=%fused_computation.110 | convolution fusion | flops 808976384 | bytes 1048576 | tf_op jit(solution)/shard_map/dot_general | solution.py:78
  137.3 5.6 %convolution_add_fusion = f32[512,256]{1,0:T(8,128)S(1)} fusion(f32[512,256]{1,0:T(8,128)S(1)} %fusion.65, f32[512,256]{1,0:T(8,128)S(1)} %get-tuple-element.175), kind=kOutput, calls=%fused_computation.32 | convolution fusion | flops 809107456 | bytes 1572864 | tf_op jit(solution)/shard_map/dot_general | solution.py:78
  142.9 7.2 %subtract_bitcast_fusion.1 = (f32[1,512,256]{2,1,0:T(8,128)S(1)}, f32[1,512,256]{2,1,0:T(8,128)S(1)}) fusion(f32[512,256]{1,0:T(8,128)S(1)} %convolution_add_fusion, f32[512]{0:T(512)S(1)} %get-tuple-element.185, f32[512]{0:T(512)S(1)} %get-tuple-element.186, f32[512,256]{1,0:T(8,128)S(1)} %fusion.63, f32[512,256]{1,0:T(8,128)S(1)} %get-tuple-element.175), kind=kOutput, calls=%fused_computation.107 | convolution fusion | flops 809893888 | bytes 2625536 | tf_op jit(solution)/shard_map/dot_general | solution.py:78
  150.2 1.8 copy.17
  152.0 7.3 %all-to-all-start = ((f32[2,1,512,256]{3,0,1,2:T(2,128)}), f32[2,1,512,256]{3,0,1,2:T(2,128)S(1)}, u32[]{:S(2)}, u32[]{:S(2)}) async-start(f32[2,1,512,256]{3,0,1,2:T(2,128)} %copy.17), calls=%async_computation | async-start | bytes 2097152 | tf_op jit(solution)/shard_map/all_to_all | solution.py:115
  159.3 25.7 %all-to-all-done = f32[2,1,512,256]{3,0,1,2:T(2,128)S(1)} async-done(((f32[2,1,512,256]{3,0,1,2:T(2,128)}), f32[2,1,512,256]{3,0,1,2:T(2,128)S(1)}, u32[]{:S(2)}, u32[]{:S(2)}) %all-to-all-start) | async-done | bytes 1048608 | tf_op jit(solution)/shard_map/all_to_all | solution.py:115
  185.0 0.8 fusion.127
  185.8 0.8 fusion.70
  186.7 0.8 fusion.72
  187.5 0.8 convolution_add_fusion.1
  188.4 1.0 add_bitcast_fusion
  189.6 1.3 collective-permute-start
  190.9 1.3 collective-permute-start.1
  192.4 2.3 %collective-permute-done.1 = f32[2,8,64,8]{3,1,2,0:T(8,128)S(1)} collective-permute-done((f32[2,8,64,8]{3,1,2,0:T(8,128)S(1)}, f32[2,8,64,8]{3,1,2,0:T(8,128)S(1)}, u32[]{:S(2)}, u32[]{:S(2)}) %collective-permute-start.1) | collective-permute-done | bytes 32800 | tf_op jit(solution)/shard_map/ppermute | solution.py:20
  195.2 4.2 %fusion.30 = (f32[2,8,64,256,1]{3,1,2,0,4:T(8,128)S(1)}, f32[2,8,64,256,1]{3,1,2,0,4:T(8,128)S(1)}) fusion(f32[1,8,64,256]{3,1,2,0:T(8,128)S(1)} %get-tuple-element.165, f32[1,8,64,256]{3,1,2,0:T(8,128)S(1)} %get-tuple-element.166, f32[2,8,64,264]{3,1,2,0:T(8,128)S(1)} %get-tuple-element.170, f32[2,8,64,264]{3,1,2,0:T(8,128)S(1)} %get-tuple-element.169), kind=kLoop, calls=%fused_computation.74 | loop fusion | flops 8388608 | bytes 18874368 | tf_op jit(solution)/shard_map/stack | solution.py:73
  199.6 3.9 %copy.24 = f32[2,8,64,256,2]{2,1,4,3,0:T(8,128)} copy(f32[2,8,64,256,2]{3,1,2,0,4:T(8,128)S(1)} %pad_maximum_fusion) | data formatting | bytes 4194304 | tf_op jit(solution)/shard_map/stack | solution.py:73
  203.5 3.8 %copy.25 = f32[2,8,64,512]{3,2,1,0:T(8,128)} copy(f32[2,8,64,512]{2,1,3,0:T(8,128)} %bitcast.51) | data formatting | bytes 4194304 | tf_op jit(solution)/shard_map/reshape | solution.py:74
  (132 shorter events, 38.2 us)
Async XLA Ops:
  152.0 33.0 %all-to-all-start = ((f32[2,1,512,256]{3,0,1,2:T(2,128)}), f32[2,1,512,256]{3,0,1,2:T(2,128)S(1)}, u32[]{:S(2)}, u32[]{:S(2)}) async-start(f32[2,1,512,256]{3,0,1,2:T(2,128)} %copy.17), calls=%async_computation | async-start | bytes 2097152 | tf_op jit(solution)/shard_map/all_to_all | solution.py:115
  189.6 2.8 %collective-permute-start = (f32[2,8,64,8]{3,1,2,0:T(8,128)S(1)}, f32[2,8,64,8]{3,1,2,0:T(8,128)S(1)}, u32[]{:S(2)}, u32[]{:S(2)}) collective-permute-start(f32[2,8,64,8]{3,1,2,0:T(8,128)S(1)} %get-tuple-element.171), channel_id=1, source_target_pairs={{0,1},{2,3},{4,5},{6,7},{8,9},{10,11},{12,13},{14,15},{16,17},{18,... | collective-permute-start | bytes 98312 | tf_op jit(solution)/shard_map/ppermute | solution.py:17
  190.9 3.8 %collective-permute-start.1 = (f32[2,8,64,8]{3,1,2,0:T(8,128)S(1)}, f32[2,8,64,8]{3,1,2,0:T(8,128)S(1)}, u32[]{:S(2)}, u32[]{:S(2)}) collective-permute-start(f32[2,8,64,8]{3,1,2,0:T(8,128)S(1)} %get-tuple-element.172), channel_id=1, source_target_pairs={{1,0},{3,2},{5,4},{7,6},{9,8},{11,10},{13,12},{15,14},{17,16},{19,... | collective-permute-start | bytes 98312 | tf_op jit(solution)/shard_map/ppermute | solution.py:20
where the time goes:
time: 210 us; the launch traced here: 207 us
  other arithmetic  129 us (61%)
  waiting for transfers between devices  28.2 us (13%)
  matrix products  27.5 us (13%)
  local copies, waits for them, and re-layouts  10.4 us (5%)
  starting transfers between devices  9.87 us (5%)
    add x32, other arithmetic, add_term(): sum_im + jnp.where(active, piece_im, 0.0)  75.7 us
    all_to_all x1, waiting for transfers between devices, per_device(): lax.all_to_all(sectioned, 'res', split_axis=2, concat_axis=1, tiled=True)  25.7 us
    dot_general x4, matrix products, matmul_high(): jnp.dot(left, right, precision=lax.Precision.HIGHEST, preferred_element_t...  24.1 us
    lt x32, other arithmetic, add_term(): active = term_index < count_row  22.4 us
    mul x32, other arithmetic, per_device(): (t_start[0] + positions).astype(jnp.float32) * time_step  20.9 us
    all_to_all x1, starting transfers between devices, per_device(): lax.all_to_all(sectioned, 'res', split_axis=2, concat_axis=1, tiled=True)  7.26 us
    another operation x2, other arithmetic, refine(): stacked = jnp.stack([coarse, middle], axis=-1)  4.36 us
  transfers between devices with their start and end apart: 3, of which 3 were waited for; matrix products, arithmetic and copies ran while one was open for 0% of the time, Pallas kernels for 0%

commit v1 on v0

--- a/solution.py
+++ b/solution.py
@@ -112,7 +112,10 @@
     turned_re = twist_cos * mixed_re - twist_sin * mixed_im
     turned_im = twist_sin * mixed_re + twist_cos * mixed_im
     sectioned = jnp.stack([turned_re, turned_im])[:, None]
-    block_in = lax.all_to_all(sectioned, "res", split_axis=2, concat_axis=1, tiled=True)
+    block_in = jnp.concatenate(
+        lax.all_to_all(jnp.stack(jnp.split(sectioned, lax.axis_size("res"), axis=2)), "res", 0, 0),
+        axis=1,
+    )
     part_re = block_in[0]
     part_im = block_in[1]
 

time: 210 us -> 213 us (1.014)
  local copies, waits for them, and re-layouts: 10.4 us -> 13.1 us
    unnamed x2 -> x7, local copies, waits for them, and re-layouts: 0.07 us -> 4.65 us
where the time goes in v1:
time: 213 us; the launch traced here: 210 us
  other arithmetic  129 us (61%)
  waiting for transfers between devices  28.2 us (13%)
  matrix products  27.5 us (13%)
  local copies, waits for them, and re-layouts  13.1 us (6%)
  starting transfers between devices  9.87 us (5%)
    add x32, other arithmetic, add_term(): sum_im + jnp.where(active, piece_im, 0.0)  75.7 us
    all_to_all x1, waiting for transfers between devices, per_device(): lax.all_to_all(jnp.stack(jnp.split(sectioned, lax.axis_size('res'), axis=...  25.7 us
    dot_general x4, matrix products, matmul_high(): jnp.dot(left, right, precision=lax.Precision.HIGHEST, preferred_element_t...  24.1 us
    lt x32, other arithmetic, add_term(): active = term_index < count_row  22.4 us
    mul x32, other arithmetic, per_device(): (t_start[0] + positions).astype(jnp.float32) * time_step  20.9 us
    all_to_all x1, starting transfers between devices, per_device(): lax.all_to_all(jnp.stack(jnp.split(sectioned, lax.axis_size('res'), axis=...  7.26 us
    unnamed x7, local copies, waits for them, and re-layouts  4.65 us
    another operation x2, other arithmetic, refine(): stacked = jnp.stack([coarse, middle], axis=-1)  4.36 us
  transfers between devices with their start and end apart: 3, of which 3 were waited for; matrix products, arithmetic and copies ran while one was open for 0% of the time, Pallas kernels for 0%

profile of v1, /device:TPU:0, one launch (start us, length us, event | category | flops | bytes accessed | tf_op | source)
XLA Modules:
  0.0 210.0 jit_solution(12155001008396109148)
XLA Ops:
  2.1 121.0 %while.16 = (s32[]{:T(128)}, f32[512,256]{1,0:T(8,128)S(1)}, f32[512,256]{1,0:T(8,128)S(1)}, s32[1,256]{1,0:T(1,128)}, f32[512,1]{0,1:T(1,128)S(1)}, /*index=5*/s32[]{:T(128)}, s32[]{:T(128)}, s32[]{:T(128)}, s32[]{:T(128)}) while((s32[]{:T(128)}, f32[512,256]{1,0:T(8,128)S(1)}, f32[512,256]{1,0:T(8,128)S(1)}, s32[1,256]{1,0:T(1,128)}, ...), condition=%wide.region_1.2_spmd.clone, body=%wide.region_0.1_spmd.clone.sunk | while | flops 1181956 | bytes 2117255 | solution.py:45
  3.4 2.4 %fusion.146 = (f32[512,256]{1,0:T(8,128)S(1)}, f32[512,256]{1,0:T(8,128)S(1)}) fusion(f32[512,256]{1,0:T(8,128)S(1)} %get-tuple-element.249, f32[512]{0:T(512)S(1)} %neg.53, f32[512]{0:T(512)S(1)} %bitcast.90, f32[256]{0:T(256)S(1)} %bitcast.91, pred[]{:T(512)S(6)} %compare.5, pred[256]{0:T(512)(128)(4,1)S(1)} %compare_reduce_fusion.2, ...), kind=kLoop, calls=%fused_computation.8.clone.1 | loop fusion | flops 1179648 | bytes 2104577 | tf_op jit(solution)/shard_map/while/body/eval_jaxpr/add | solution.py:41
  5.8 0.7 compare_reduce_fusion.2
  7.2 2.4 %fusion.146 = (f32[512,256]{1,0:T(8,128)S(1)}, f32[512,256]{1,0:T(8,128)S(1)}) fusion(f32[512,256]{1,0:T(8,128)S(1)} %get-tuple-element.249, f32[512]{0:T(512)S(1)} %neg.53, f32[512]{0:T(512)S(1)} %bitcast.90, f32[256]{0:T(256)S(1)} %bitcast.91, pred[]{:T(512)S(6)} %compare.5, pred[256]{0:T(512)(128)(4,1)S(1)} %compare_reduce_fusion.2, ...), kind=kLoop, calls=%fused_computation.8.clone.1 | loop fusion | flops 1179648 | bytes 2104577 | tf_op jit(solution)/shard_map/while/body/eval_jaxpr/add | solution.py:41
  9.6 0.7 compare_reduce_fusion.2
  11.0 2.4 %fusion.146 = (f32[512,256]{1,0:T(8,128)S(1)}, f32[512,256]{1,0:T(8,128)S(1)}) fusion(f32[512,256]{1,0:T(8,128)S(1)} %get-tuple-element.249, f32[512]{0:T(512)S(1)} %neg.53, f32[512]{0:T(512)S(1)} %bitcast.90, f32[256]{0:T(256)S(1)} %bitcast.91, pred[]{:T(512)S(6)} %compare.5, pred[256]{0:T(512)(128)(4,1)S(1)} %compare_reduce_fusion.2, ...), kind=kLoop, calls=%fused_computation.8.clone.1 | loop fusion | flops 1179648 | bytes 2104577 | tf_op jit(solution)/shard_map/while/body/eval_jaxpr/add | solution.py:41
  13.4 0.7 compare_reduce_fusion.2
  14.8 2.4 %fusion.146 = (f32[512,256]{1,0:T(8,128)S(1)}, f32[512,256]{1,0:T(8,128)S(1)}) fusion(f32[512,256]{1,0:T(8,128)S(1)} %get-tuple-element.249, f32[512]{0:T(512)S(1)} %neg.53, f32[512]{0:T(512)S(1)} %bitcast.90, f32[256]{0:T(256)S(1)} %bitcast.91, pred[]{:T(512)S(6)} %compare.5, pred[256]{0:T(512)(128)(4,1)S(1)} %compare_reduce_fusion.2, ...), kind=kLoop, calls=%fused_computation.8.clone.1 | loop fusion | flops 1179648 | bytes 2104577 | tf_op jit(solution)/shard_map/while/body/eval_jaxpr/add | solution.py:41
  17.2 0.7 compare_reduce_fusion.2
  18.6 2.4 %fusion.146 = (f32[512,256]{1,0:T(8,128)S(1)}, f32[512,256]{1,0:T(8,128)S(1)}) fusion(f32[512,256]{1,0:T(8,128)S(1)} %get-tuple-element.249, f32[512]{0:T(512)S(1)} %neg.53, f32[512]{0:T(512)S(1)} %bitcast.90, f32[256]{0:T(256)S(1)} %bitcast.91, pred[]{:T(512)S(6)} %compare.5, pred[256]{0:T(512)(128)(4,1)S(1)} %compare_reduce_fusion.2, ...), kind=kLoop, calls=%fused_computation.8.clone.1 | loop fusion | flops 1179648 | bytes 2104577 | tf_op jit(solution)/shard_map/while/body/eval_jaxpr/add | solution.py:41
  21.0 0.7 compare_reduce_fusion.2
  22.4 2.4 %fusion.146 = (f32[512,256]{1,0:T(8,128)S(1)}, f32[512,256]{1,0:T(8,128)S(1)}) fusion(f32[512,256]{1,0:T(8,128)S(1)} %get-tuple-element.249, f32[512]{0:T(512)S(1)} %neg.53, f32[512]{0:T(512)S(1)} %bitcast.90, f32[256]{0:T(256)S(1)} %bitcast.91, pred[]{:T(512)S(6)} %compare.5, pred[256]{0:T(512)(128)(4,1)S(1)} %compare_reduce_fusion.2, ...), kind=kLoop, calls=%fused_computation.8.clone.1 | loop fusion | flops 1179648 | bytes 2104577 | tf_op jit(solution)/shard_map/while/body/eval_jaxpr/add | solution.py:41
  24.8 0.7 compare_reduce_fusion.2
  26.1 2.4 %fusion.146 = (f32[512,256]{1,0:T(8,128)S(1)}, f32[512,256]{1,0:T(8,128)S(1)}) fusion(f32[512,256]{1,0:T(8,128)S(1)} %get-tuple-element.249, f32[512]{0:T(512)S(1)} %neg.53, f32[512]{0:T(512)S(1)} %bitcast.90, f32[256]{0:T(256)S(1)} %bitcast.91, pred[]{:T(512)S(6)} %compare.5, pred[256]{0:T(512)(128)(4,1)S(1)} %compare_reduce_fusion.2, ...), kind=kLoop, calls=%fused_computation.8.clone.1 | loop fusion | flops 1179648 | bytes 2104577 | tf_op jit(solution)/shard_map/while/body/eval_jaxpr/add | solution.py:41
  29.9 2.4 %fusion.146 = (f32[512,256]{1,0:T(8,128)S(1)}, f32[512,256]{1,0:T(8,128)S(1)}) fusion(f32[512,256]{1,0:T(8,128)S(1)} %get-tuple-element.249, f32[512]{0:T(512)S(1)} %neg.53, f32[512]{0:T(512)S(1)} %bitcast.90, f32[256]{0:T(256)S(1)} %bitcast.91, pred[]{:T(512)S(6)} %compare.5, pred[256]{0:T(512)(128)(4,1)S(1)} %compare_reduce_fusion.2, ...), kind=kLoop, calls=%fused_computation.8.clone.1 | loop fusion | flops 1179648 | bytes 2104577 | tf_op jit(solution)/shard_map/while/body/eval_jaxpr/add | solution.py:41
  33.7 2.4 %fusion.146 = (f32[512,256]{1,0:T(8,128)S(1)}, f32[512,256]{1,0:T(8,128)S(1)}) fusion(f32[512,256]{1,0:T(8,128)S(1)} %get-tuple-element.249, f32[512]{0:T(512)S(1)} %neg.53, f32[512]{0:T(512)S(1)} %bitcast.90, f32[256]{0:T(256)S(1)} %bitcast.91, pred[]{:T(512)S(6)} %compare.5, pred[256]{0:T(512)(128)(4,1)S(1)} %compare_reduce_fusion.2, ...), kind=kLoop, calls=%fused_computation.8.clone.1 | loop fusion | flops 1179648 | bytes 2104577 | tf_op jit(solution)/shard_map/while/body/eval_jaxpr/add | solution.py:41
  37.5 2.4 %fusion.146 = (f32[512,256]{1,0:T(8,128)S(1)}, f32[512,256]{1,0:T(8,128)S(1)}) fusion(f32[512,256]{1,0:T(8,128)S(1)} %get-tuple-element.249, f32[512]{0:T(512)S(1)} %neg.53, f32[512]{0:T(512)S(1)} %bitcast.90, f32[256]{0:T(256)S(1)} %bitcast.91, pred[]{:T(512)S(6)} %compare.5, pred[256]{0:T(512)(128)(4,1)S(1)} %compare_reduce_fusion.2, ...), kind=kLoop, calls=%fused_computation.8.clone.1 | loop fusion | flops 1179648 | bytes 2104577 | tf_op jit(solution)/shard_map/while/body/eval_jaxpr/add | solution.py:41
  39.9 0.7 compare_reduce_fusion.2
  41.3 2.4 %fusion.146 = (f32[512,256]{1,0:T(8,128)S(1)}, f32[512,256]{1,0:T(8,128)S(1)}) fusion(f32[512,256]{1,0:T(8,128)S(1)} %get-tuple-element.249, f32[512]{0:T(512)S(1)} %neg.53, f32[512]{0:T(512)S(1)} %bitcast.90, f32[256]{0:T(256)S(1)} %bitcast.91, pred[]{:T(512)S(6)} %compare.5, pred[256]{0:T(512)(128)(4,1)S(1)} %compare_reduce_fusion.2, ...), kind=kLoop, calls=%fused_computation.8.clone.1 | loop fusion | flops 1179648 | bytes 2104577 | tf_op jit(solution)/shard_map/while/body/eval_jaxpr/add | solution.py:41
  45.1 2.4 %fusion.146 = (f32[512,256]{1,0:T(8,128)S(1)}, f32[512,256]{1,0:T(8,128)S(1)}) fusion(f32[512,256]{1,0:T(8,128)S(1)} %get-tuple-element.249, f32[512]{0:T(512)S(1)} %neg.53, f32[512]{0:T(512)S(1)} %bitcast.90, f32[256]{0:T(256)S(1)} %bitcast.91, pred[]{:T(512)S(6)} %compare.5, pred[256]{0:T(512)(128)(4,1)S(1)} %compare_reduce_fusion.2, ...), kind=kLoop, calls=%fused_computation.8.clone.1 | loop fusion | flops 1179648 | bytes 2104577 | tf_op jit(solution)/shard_map/while/body/eval_jaxpr/add | solution.py:41
  47.4 0.7 compare_reduce_fusion.2
  48.8 2.4 %fusion.146 = (f32[512,256]{1,0:T(8,128)S(1)}, f32[512,256]{1,0:T(8,128)S(1)}) fusion(f32[512,256]{1,0:T(8,128)S(1)} %get-tuple-element.249, f32[512]{0:T(512)S(1)} %neg.53, f32[512]{0:T(512)S(1)} %bitcast.90, f32[256]{0:T(256)S(1)} %bitcast.91, pred[]{:T(512)S(6)} %compare.5, pred[256]{0:T(512)(128)(4,1)S(1)} %compare_reduce_fusion.2, ...), kind=kLoop, calls=%fused_computation.8.clone.1 | loop fusion | flops 1179648 | bytes 2104577 | tf_op jit(solution)/shard_map/while/body/eval_jaxpr/add | solution.py:41
  52.6 2.4 %fusion.146 = (f32[512,256]{1,0:T(8,128)S(1)}, f32[512,256]{1,0:T(8,128)S(1)}) fusion(f32[512,256]{1,0:T(8,128)S(1)} %get-tuple-element.249, f32[512]{0:T(512)S(1)} %neg.53, f32[512]{0:T(512)S(1)} %bitcast.90, f32[256]{0:T(256)S(1)} %bitcast.91, pred[]{:T(512)S(6)} %compare.5, pred[256]{0:T(512)(128)(4,1)S(1)} %compare_reduce_fusion.2, ...), kind=kLoop, calls=%fused_computation.8.clone.1 | loop fusion | flops 1179648 | bytes 2104577 | tf_op jit(solution)/shard_map/while/body/eval_jaxpr/add | solution.py:41
  56.4 2.4 %fusion.146 = (f32[512,256]{1,0:T(8,128)S(1)}, f32[512,256]{1,0:T(8,128)S(1)}) fusion(f32[512,256]{1,0:T(8,128)S(1)} %get-tuple-element.249, f32[512]{0:T(512)S(1)} %neg.53, f32[512]{0:T(512)S(1)} %bitcast.90, f32[256]{0:T(256)S(1)} %bitcast.91, pred[]{:T(512)S(6)} %compare.5, pred[256]{0:T(512)(128)(4,1)S(1)} %compare_reduce_fusion.2, ...), kind=kLoop, calls=%fused_computation.8.clone.1 | loop fusion | flops 1179648 | bytes 2104577 | tf_op jit(solution)/shard_map/while/body/eval_jaxpr/add | solution.py:41
  58.8 0.7 compare_reduce_fusion.2
  60.2 2.4 %fusion.146 = (f32[512,256]{1,0:T(8,128)S(1)}, f32[512,256]{1,0:T(8,128)S(1)}) fusion(f32[512,256]{1,0:T(8,128)S(1)} %get-tuple-element.249, f32[512]{0:T(512)S(1)} %neg.53, f32[512]{0:T(512)S(1)} %bitcast.90, f32[256]{0:T(256)S(1)} %bitcast.91, pred[]{:T(512)S(6)} %compare.5, pred[256]{0:T(512)(128)(4,1)S(1)} %compare_reduce_fusion.2, ...), kind=kLoop, calls=%fused_computation.8.clone.1 | loop fusion | flops 1179648 | bytes 2104577 | tf_op jit(solution)/shard_map/while/body/eval_jaxpr/add | solution.py:41
  64.0 2.4 %fusion.146 = (f32[512,256]{1,0:T(8,128)S(1)}, f32[512,256]{1,0:T(8,128)S(1)}) fusion(f32[512,256]{1,0:T(8,128)S(1)} %get-tuple-element.249, f32[512]{0:T(512)S(1)} %neg.53, f32[512]{0:T(512)S(1)} %bitcast.90, f32[256]{0:T(256)S(1)} %bitcast.91, pred[]{:T(512)S(6)} %compare.5, pred[256]{0:T(512)(128)(4,1)S(1)} %compare_reduce_fusion.2, ...), kind=kLoop, calls=%fused_computation.8.clone.1 | loop fusion | flops 1179648 | bytes 2104577 | tf_op jit(solution)/shard_map/while/body/eval_jaxpr/add | solution.py:41
  66.4 0.7 compare_reduce_fusion.2
  67.8 2.4 %fusion.146 = (f32[512,256]{1,0:T(8,128)S(1)}, f32[512,256]{1,0:T(8,128)S(1)}) fusion(f32[512,256]{1,0:T(8,128)S(1)} %get-tuple-element.249, f32[512]{0:T(512)S(1)} %neg.53, f32[512]{0:T(512)S(1)} %bitcast.90, f32[256]{0:T(256)S(1)} %bitcast.91, pred[]{:T(512)S(6)} %compare.5, pred[256]{0:T(512)(128)(4,1)S(1)} %compare_reduce_fusion.2, ...), kind=kLoop, calls=%fused_computation.8.clone.1 | loop fusion | flops 1179648 | bytes 2104577 | tf_op jit(solution)/shard_map/while/body/eval_jaxpr/add | solution.py:41
  71.5 2.4 %fusion.146 = (f32[512,256]{1,0:T(8,128)S(1)}, f32[512,256]{1,0:T(8,128)S(1)}) fusion(f32[512,256]{1,0:T(8,128)S(1)} %get-tuple-element.249, f32[512]{0:T(512)S(1)} %neg.53, f32[512]{0:T(512)S(1)} %bitcast.90, f32[256]{0:T(256)S(1)} %bitcast.91, pred[]{:T(512)S(6)} %compare.5, pred[256]{0:T(512)(128)(4,1)S(1)} %compare_reduce_fusion.2, ...), kind=kLoop, calls=%fused_computation.8.clone.1 | loop fusion | flops 1179648 | bytes 2104577 | tf_op jit(solution)/shard_map/while/body/eval_jaxpr/add | solution.py:41
  75.3 2.4 %fusion.146 = (f32[512,256]{1,0:T(8,128)S(1)}, f32[512,256]{1,0:T(8,128)S(1)}) fusion(f32[512,256]{1,0:T(8,128)S(1)} %get-tuple-element.249, f32[512]{0:T(512)S(1)} %neg.53, f32[512]{0:T(512)S(1)} %bitcast.90, f32[256]{0:T(256)S(1)} %bitcast.91, pred[]{:T(512)S(6)} %compare.5, pred[256]{0:T(512)(128)(4,1)S(1)} %compare_reduce_fusion.2, ...), kind=kLoop, calls=%fused_computation.8.clone.1 | loop fusion | flops 1179648 | bytes 2104577 | tf_op jit(solution)/shard_map/while/body/eval_jaxpr/add | solution.py:41
  79.1 2.4 %fusion.146 = (f32[512,256]{1,0:T(8,128)S(1)}, f32[512,256]{1,0:T(8,128)S(1)}) fusion(f32[512,256]{1,0:T(8,128)S(1)} %get-tuple-element.249, f32[512]{0:T(512)S(1)} %neg.53, f32[512]{0:T(512)S(1)} %bitcast.90, f32[256]{0:T(256)S(1)} %bitcast.91, pred[]{:T(512)S(6)} %compare.5, pred[256]{0:T(512)(128)(4,1)S(1)} %compare_reduce_fusion.2, ...), kind=kLoop, calls=%fused_computation.8.clone.1 | loop fusion | flops 1179648 | bytes 2104577 | tf_op jit(solution)/shard_map/while/body/eval_jaxpr/add | solution.py:41
  82.9 2.4 %fusion.146 = (f32[512,256]{1,0:T(8,128)S(1)}, f32[512,256]{1,0:T(8,128)S(1)}) fusion(f32[512,256]{1,0:T(8,128)S(1)} %get-tuple-element.249, f32[512]{0:T(512)S(1)} %neg.53, f32[512]{0:T(512)S(1)} %bitcast.90, f32[256]{0:T(256)S(1)} %bitcast.91, pred[]{:T(512)S(6)} %compare.5, pred[256]{0:T(512)(128)(4,1)S(1)} %compare_reduce_fusion.2, ...), kind=kLoop, calls=%fused_computation.8.clone.1 | loop fusion | flops 1179648 | bytes 2104577 | tf_op jit(solution)/shard_map/while/body/eval_jaxpr/add | solution.py:41
  85.3 0.7 compare_reduce_fusion.2
  86.7 2.4 %fusion.146 = (f32[512,256]{1,0:T(8,128)S(1)}, f32[512,256]{1,0:T(8,128)S(1)}) fusion(f32[512,256]{1,0:T(8,128)S(1)} %get-tuple-element.249, f32[512]{0:T(512)S(1)} %neg.53, f32[512]{0:T(512)S(1)} %bitcast.90, f32[256]{0:T(256)S(1)} %bitcast.91, pred[]{:T(512)S(6)} %compare.5, pred[256]{0:T(512)(128)(4,1)S(1)} %compare_reduce_fusion.2, ...), kind=kLoop, calls=%fused_computation.8.clone.1 | loop fusion | flops 1179648 | bytes 2104577 | tf_op jit(solution)/shard_map/while/body/eval_jaxpr/add | solution.py:41
  90.4 2.4 %fusion.146 = (f32[512,256]{1,0:T(8,128)S(1)}, f32[512,256]{1,0:T(8,128)S(1)}) fusion(f32[512,256]{1,0:T(8,128)S(1)} %get-tuple-element.249, f32[512]{0:T(512)S(1)} %neg.53, f32[512]{0:T(512)S(1)} %bitcast.90, f32[256]{0:T(256)S(1)} %bitcast.91, pred[]{:T(512)S(6)} %compare.5, pred[256]{0:T(512)(128)(4,1)S(1)} %compare_reduce_fusion.2, ...), kind=kLoop, calls=%fused_computation.8.clone.1 | loop fusion | flops 1179648 | bytes 2104577 | tf_op jit(solution)/shard_map/while/body/eval_jaxpr/add | solution.py:41
  92.8 0.7 compare_reduce_fusion.2
  94.2 2.4 %fusion.146 = (f32[512,256]{1,0:T(8,128)S(1)}, f32[512,256]{1,0:T(8,128)S(1)}) fusion(f32[512,256]{1,0:T(8,128)S(1)} %get-tuple-element.249, f32[512]{0:T(512)S(1)} %neg.53, f32[512]{0:T(512)S(1)} %bitcast.90, f32[256]{0:T(256)S(1)} %bitcast.91, pred[]{:T(512)S(6)} %compare.5, pred[256]{0:T(512)(128)(4,1)S(1)} %compare_reduce_fusion.2, ...), kind=kLoop, calls=%fused_computation.8.clone.1 | loop fusion | flops 1179648 | bytes 2104577 | tf_op jit(solution)/shard_map/while/body/eval_jaxpr/add | solution.py:41
  98.0 2.4 %fusion.146 = (f32[512,256]{1,0:T(8,128)S(1)}, f32[512,256]{1,0:T(8,128)S(1)}) fusion(f32[512,256]{1,0:T(8,128)S(1)} %get-tuple-element.249, f32[512]{0:T(512)S(1)} %neg.53, f32[512]{0:T(512)S(1)} %bitcast.90, f32[256]{0:T(256)S(1)} %bitcast.91, pred[]{:T(512)S(6)} %compare.5, pred[256]{0:T(512)(128)(4,1)S(1)} %compare_reduce_fusion.2, ...), kind=kLoop, calls=%fused_computation.8.clone.1 | loop fusion | flops 1179648 | bytes 2104577 | tf_op jit(solution)/shard_map/while/body/eval_jaxpr/add | solution.py:41
  101.8 2.4 %fusion.146 = (f32[512,256]{1,0:T(8,128)S(1)}, f32[512,256]{1,0:T(8,128)S(1)}) fusion(f32[512,256]{1,0:T(8,128)S(1)} %get-tuple-element.249, f32[512]{0:T(512)S(1)} %neg.53, f32[512]{0:T(512)S(1)} %bitcast.90, f32[256]{0:T(256)S(1)} %bitcast.91, pred[]{:T(512)S(6)} %compare.5, pred[256]{0:T(512)(128)(4,1)S(1)} %compare_reduce_fusion.2, ...), kind=kLoop, calls=%fused_computation.8.clone.1 | loop fusion | flops 1179648 | bytes 2104577 | tf_op jit(solution)/shard_map/while/body/eval_jaxpr/add | solution.py:41
  105.6 2.4 %fusion.146 = (f32[512,256]{1,0:T(8,128)S(1)}, f32[512,256]{1,0:T(8,128)S(1)}) fusion(f32[512,256]{1,0:T(8,128)S(1)} %get-tuple-element.249, f32[512]{0:T(512)S(1)} %neg.53, f32[512]{0:T(512)S(1)} %bitcast.90, f32[256]{0:T(256)S(1)} %bitcast.91, pred[]{:T(512)S(6)} %compare.5, pred[256]{0:T(512)(128)(4,1)S(1)} %compare_reduce_fusion.2, ...), kind=kLoop, calls=%fused_computation.8.clone.1 | loop fusion | flops 1179648 | bytes 2104577 | tf_op jit(solution)/shard_map/while/body/eval_jaxpr/add | solution.py:41
  109.4 2.4 %fusion.146 = (f32[512,256]{1,0:T(8,128)S(1)}, f32[512,256]{1,0:T(8,128)S(1)}) fusion(f32[512,256]{1,0:T(8,128)S(1)} %get-tuple-element.249, f32[512]{0:T(512)S(1)} %neg.53, f32[512]{0:T(512)S(1)} %bitcast.90, f32[256]{0:T(256)S(1)} %bitcast.91, pred[]{:T(512)S(6)} %compare.5, pred[256]{0:T(512)(128)(4,1)S(1)} %compare_reduce_fusion.2, ...), kind=kLoop, calls=%fused_computation.8.clone.1 | loop fusion | flops 1179648 | bytes 2104577 | tf_op jit(solution)/shard_map/while/body/eval_jaxpr/add | solution.py:41
  111.8 0.7 compare_reduce_fusion.2
  113.1 2.4 %fusion.146 = (f32[512,256]{1,0:T(8,128)S(1)}, f32[512,256]{1,0:T(8,128)S(1)}) fusion(f32[512,256]{1,0:T(8,128)S(1)} %get-tuple-element.249, f32[512]{0:T(512)S(1)} %neg.53, f32[512]{0:T(512)S(1)} %bitcast.90, f32[256]{0:T(256)S(1)} %bitcast.91, pred[]{:T(512)S(6)} %compare.5, pred[256]{0:T(512)(128)(4,1)S(1)} %compare_reduce_fusion.2, ...), kind=kLoop, calls=%fused_computation.8.clone.1 | loop fusion | flops 1179648 | bytes 2104577 | tf_op jit(solution)/shard_map/while/body/eval_jaxpr/add | solution.py:41
  116.9 2.4 %fusion.146 = (f32[512,256]{1,0:T(8,128)S(1)}, f32[512,256]{1,0:T(8,128)S(1)}) fusion(f32[512,256]{1,0:T(8,128)S(1)} %get-tuple-element.249, f32[512]{0:T(512)S(1)} %neg.53, f32[512]{0:T(512)S(1)} %bitcast.90, f32[256]{0:T(256)S(1)} %bitcast.91, pred[]{:T(512)S(6)} %compare.5, pred[256]{0:T(512)(128)(4,1)S(1)} %compare_reduce_fusion.2, ...), kind=kLoop, calls=%fused_computation.8.clone.1 | loop fusion | flops 1179648 | bytes 2104577 | tf_op jit(solution)/shard_map/while/body/eval_jaxpr/add | solution.py:41
  119.3 0.7 compare_reduce_fusion.2
  120.7 2.4 %fusion.146 = (f32[512,256]{1,0:T(8,128)S(1)}, f32[512,256]{1,0:T(8,128)S(1)}) fusion(f32[512,256]{1,0:T(8,128)S(1)} %get-tuple-element.249, f32[512]{0:T(512)S(1)} %neg.53, f32[512]{0:T(512)S(1)} %bitcast.90, f32[256]{0:T(256)S(1)} %bitcast.91, pred[]{:T(512)S(6)} %compare.5, pred[256]{0:T(512)(128)(4,1)S(1)} %compare_reduce_fusion.2, ...), kind=kLoop, calls=%fused_computation.8.clone.1 | loop fusion | flops 1179648 | bytes 2104577 | tf_op jit(solution)/shard_map/while/body/eval_jaxpr/add | solution.py:41
  123.1 2.9 %fusion.38 = (f32[512,256]{1,0:T(8,128)S(1)}, f32[512,256]{1,0:T(8,128)S(1)}) fusion(f32[512,256]{1,0:T(8,128)S(1)} %get-tuple-element.116, f32[256]{0:T(256)S(1)} %fusion.101, f32[256]{0:T(256)S(1)} %get-tuple-element.180, f32[256]{0:T(256)S(1)} %get-tuple-element.183, f32[256]{0:T(256)S(1)} %get-tuple-element.179, f32[256]{0:T(256)S(1)} %get-tuple-element.184, ...), kind=kLoop, calls=%fused_computation.82 | loop fusion | flops 5636096 | bytes 2105344 | tf_op jit(solution)/shard_map/sub | solution.py:59
  126.0 5.6 %fusion.65 = f32[512,256]{1,0:T(8,128)S(1)} fusion(f32[512,256]{1,0:T(8,128)S(1)} %get-tuple-element.176), kind=kOutput, calls=%fused_computation.113 | convolution fusion | flops 808976384 | bytes 1048576 | tf_op jit(solution)/shard_map/dot_general | solution.py:78
  131.6 5.6 %fusion.63 = f32[512,256]{1,0:T(8,128)S(1)} fusion(f32[512,256]{1,0:T(8,128)S(1)} %get-tuple-element.176), kind=kOutput, calls=%fused_computation.112 | convolution fusion | flops 808976384 | bytes 1048576 | tf_op jit(solution)/shard_map/dot_general | solution.py:78
  137.3 5.6 %convolution_add_fusion = f32[512,256]{1,0:T(8,128)S(1)} fusion(f32[512,256]{1,0:T(8,128)S(1)} %fusion.65, f32[512,256]{1,0:T(8,128)S(1)} %get-tuple-element.175), kind=kOutput, calls=%fused_computation.32 | convolution fusion | flops 809107456 | bytes 1572864 | tf_op jit(solution)/shard_map/dot_general | solution.py:78
  142.9 7.2 %subtract_bitcast_fusion.1 = (f32[1,512,256]{2,1,0:T(8,128)S(1)}, f32[1,512,256]{2,1,0:T(8,128)S(1)}) fusion(f32[512,256]{1,0:T(8,128)S(1)} %convolution_add_fusion, f32[512]{0:T(512)S(1)} %get-tuple-element.185, f32[512]{0:T(512)S(1)} %get-tuple-element.186, f32[512,256]{1,0:T(8,128)S(1)} %fusion.63, f32[512,256]{1,0:T(8,128)S(1)} %get-tuple-element.175), kind=kOutput, calls=%fused_computation.109 | convolution fusion | flops 809893888 | bytes 2625536 | tf_op jit(solution)/shard_map/dot_general | solution.py:78
  155.5 7.3 %all-to-all-start = ((f32[8,2,1,64,256]{4,3,1,2,0:T(8,128)}), f32[8,2,1,64,256]{4,3,1,2,0:T(8,128)S(1)}, u32[]{:S(2)}, u32[]{:S(2)}) async-start(f32[8,2,1,64,256]{4,3,1,2,0:T(8,128)} %fusion.74), calls=%async_computation | async-start | bytes 2097152 | tf_op jit(solution)/shard_map/all_to_all | solution.py:116
  162.8 25.7 %all-to-all-done = f32[8,2,1,64,256]{4,3,1,2,0:T(8,128)S(1)} async-done(((f32[8,2,1,64,256]{4,3,1,2,0:T(8,128)}), f32[8,2,1,64,256]{4,3,1,2,0:T(8,128)S(1)}, u32[]{:S(2)}, u32[]{:S(2)}) %all-to-all-start) | async-done | bytes 1048608 | tf_op jit(solution)/shard_map/all_to_all | solution.py:116
  188.6 0.8 fusion.70
  189.4 0.8 fusion.72
  190.3 0.8 convolution_add_fusion.1
  191.1 1.0 add_bitcast_fusion
  192.3 1.3 collective-permute-start
  193.6 1.3 collective-permute-start.1
  195.1 2.3 %collective-permute-done.1 = f32[2,8,64,8]{3,1,2,0:T(8,128)S(1)} collective-permute-done((f32[2,8,64,8]{3,1,2,0:T(8,128)S(1)}, f32[2,8,64,8]{3,1,2,0:T(8,128)S(1)}, u32[]{:S(2)}, u32[]{:S(2)}) %collective-permute-start.1) | collective-permute-done | bytes 32800 | tf_op jit(solution)/shard_map/ppermute | solution.py:20
  197.9 4.2 %fusion.30 = (f32[2,8,64,256,1]{3,1,2,0,4:T(8,128)S(1)}, f32[2,8,64,256,1]{3,1,2,0,4:T(8,128)S(1)}) fusion(f32[1,8,64,256]{3,1,2,0:T(8,128)S(1)} %get-tuple-element.165, f32[1,8,64,256]{3,1,2,0:T(8,128)S(1)} %get-tuple-element.166, f32[2,8,64,264]{3,1,2,0:T(8,128)S(1)} %get-tuple-element.170, f32[2,8,64,264]{3,1,2,0:T(8,128)S(1)} %get-tuple-element.169), kind=kLoop, calls=%fused_computation.74 | loop fusion | flops 8388608 | bytes 18874368 | tf_op jit(solution)/shard_map/stack | solution.py:73
  202.3 3.9 %copy.12 = f32[2,8,64,256,2]{2,1,4,3,0:T(8,128)} copy(f32[2,8,64,256,2]{3,1,2,0,4:T(8,128)S(1)} %pad_maximum_fusion) | data formatting | bytes 4194304 | tf_op jit(solution)/shard_map/stack | solution.py:73
  206.2 3.8 %copy.13 = f32[2,8,64,512]{3,2,1,0:T(8,128)} copy(f32[2,8,64,512]{2,1,3,0:T(8,128)} %bitcast.86) | data formatting | bytes 4194304 | tf_op jit(solution)/shard_map/reshape | solution.py:74
  (137 shorter events, 42.1 us)
Async XLA Ops:
  155.5 33.0 %all-to-all-start = ((f32[8,2,1,64,256]{4,3,1,2,0:T(8,128)}), f32[8,2,1,64,256]{4,3,1,2,0:T(8,128)S(1)}, u32[]{:S(2)}, u32[]{:S(2)}) async-start(f32[8,2,1,64,256]{4,3,1,2,0:T(8,128)} %fusion.74), calls=%async_computation | async-start | bytes 2097152 | tf_op jit(solution)/shard_map/all_to_all | solution.py:116
  192.3 2.8 %collective-permute-start = (f32[2,8,64,8]{3,1,2,0:T(8,128)S(1)}, f32[2,8,64,8]{3,1,2,0:T(8,128)S(1)}, u32[]{:S(2)}, u32[]{:S(2)}) collective-permute-start(f32[2,8,64,8]{3,1,2,0:T(8,128)S(1)} %get-tuple-element.171), channel_id=1, source_target_pairs={{0,1},{2,3},{4,5},{6,7},{8,9},{10,11},{12,13},{14,15},{16,17},{18,... | collective-permute-start | bytes 98312 | tf_op jit(solution)/shard_map/ppermute | solution.py:17
  193.6 3.8 %collective-permute-start.1 = (f32[2,8,64,8]{3,1,2,0:T(8,128)S(1)}, f32[2,8,64,8]{3,1,2,0:T(8,128)S(1)}, u32[]{:S(2)}, u32[]{:S(2)}) collective-permute-start(f32[2,8,64,8]{3,1,2,0:T(8,128)S(1)} %get-tuple-element.172), channel_id=1, source_target_pairs={{1,0},{3,2},{5,4},{7,6},{9,8},{11,10},{13,12},{15,14},{17,16},{19,... | collective-permute-start | bytes 98312 | tf_op jit(solution)/shard_map/ppermute | solution.py:20
